TPU v7x, 256 devices: a whole 4x4x8 slice. The times are simulated.
256 devices in a mesh: fsdp: 16 (over x, y_lo, core), tensor: 16 (over y_hi, z).
Axes of the slice: x: 4, y: 4 (y_hi: 2, y_lo: 2; y = y_hi * 2 + y_lo), z: 8, core: 2. Of those that a mesh axis runs over, the one named last changes fastest.
Arguments:
- queries: bfloat16 [8192, 6144], P('fsdp', 'tensor'), may hold values from -6 to 6
- keys: bfloat16 [8192, 6144], P('fsdp', 'tensor'), may hold values from -12 to 12
- values: bfloat16 [8192, 6144], P('fsdp', 'tensor'), may hold values from -6 to 6
- grad_out: bfloat16 [8192, 6144], P('fsdp', 'tensor'), may hold values from -6 to 6
- out_weight: bfloat16 [6144, 6144], P('fsdp', 'tensor'), may hold values from -0.078125 to 0.078125
Outputs:
- d_queries: bfloat16 [8192, 6144], P('fsdp', 'tensor')
- d_keys: bfloat16 [8192, 6144], P('fsdp', 'tensor')
- d_values: bfloat16 [8192, 6144], P('fsdp', 'tensor')
- d_weight: float32 [6144, 6144], P('fsdp', 'tensor')
All inputs are finite; a program needn't handle non-finite values.
Results may differ from a plain program's by a relative error of at most 0.0079.
Values may be sent and summed in bfloat16 or wider, within the bound.
A program may use at most 128 MiB of HBM per device.

v0:
```python
import jax
import jax.numpy as jnp
from jax import lax
from jax.sharding import PartitionSpec as P

HEAD_DIM = 128


def block_probs(query_block, key_heads):
    score_scale = HEAD_DIM ** (-0.5)
    scores = (
        jnp.einsum("qhe,khe->hqk", query_block, key_heads, preferred_element_type=jnp.float32)
        * score_scale
    )
    row_max = jnp.max(scores, axis=-1, keepdims=True)
    exponent = jnp.exp(scores - row_max)
    probs = exponent / jnp.sum(exponent, axis=-1, keepdims=True)
    return (probs, probs.astype(jnp.bfloat16))


def block_output(prob_rounded, value_heads):
    return jnp.einsum(
        "hqk,khe->qhe", prob_rounded, value_heads, preferred_element_type=jnp.float32
    ).astype(jnp.bfloat16)


def backward_pass(query_heads, key_heads, value_heads, grad_heads):
    score_scale = HEAD_DIM ** (-0.5)
    probs, prob_rounded = block_probs(query_heads, key_heads)
    output_blocks = [block_output(prob_rounded, value_heads)]
    grad_probs = jnp.einsum(
        "qhe,khe->hqk", grad_heads, value_heads, preferred_element_type=jnp.float32
    )
    row_dot = jnp.sum(probs * grad_probs, axis=-1, keepdims=True)
    grad_scores = (probs * (grad_probs - row_dot) * score_scale).astype(jnp.bfloat16)
    query_grads = [
        jnp.einsum(
            "hqk,khe->qhe", grad_scores, key_heads, preferred_element_type=jnp.float32
        ).astype(jnp.bfloat16)
    ]
    key_acc = jnp.einsum(
        "hqk,qhe->khe", grad_scores, query_heads, preferred_element_type=jnp.float32
    )
    value_acc = jnp.einsum(
        "hqk,qhe->khe", prob_rounded, grad_heads, preferred_element_type=jnp.float32
    )
    return (
        query_grads,
        key_acc.astype(jnp.bfloat16),
        value_acc.astype(jnp.bfloat16),
        output_blocks,
    )


def shards(queries, keys, values, grad_out, out_weight):
    seq_len = queries.shape[0]
    heads_dev = queries.shape[1] // HEAD_DIM
    query_heads = queries.reshape(seq_len, heads_dev, HEAD_DIM)
    key_heads = keys.reshape(seq_len, heads_dev, HEAD_DIM)
    value_heads = values.reshape(seq_len, heads_dev, HEAD_DIM)
    full_grad = lax.all_gather(grad_out, "tensor", axis=1, tiled=True)
    whole_weight = lax.all_gather(out_weight, "fsdp", axis=0, tiled=True)
    d_attended = jnp.dot(full_grad, whole_weight, preferred_element_type=jnp.float32)
    grad_heads = d_attended.astype(jnp.bfloat16).reshape(seq_len, heads_dev, HEAD_DIM)
    query_grads, d_keys, d_values, output_blocks = backward_pass(
        query_heads, key_heads, value_heads, grad_heads
    )
    attended = output_blocks[0].reshape(seq_len, heads_dev * HEAD_DIM)
    d_weight = lax.psum_scatter(
        lax.dot_general(
            full_grad, attended, (((0,), (0,)), ((), ())), preferred_element_type=jnp.float32
        ),
        "fsdp",
        scatter_dimension=0,
        tiled=True,
    )
    d_queries = query_grads[0].reshape(seq_len, heads_dev * HEAD_DIM)
    return (
        d_queries,
        d_keys.reshape(seq_len, heads_dev * HEAD_DIM),
        d_values.reshape(seq_len, heads_dev * HEAD_DIM),
        d_weight,
    )


def solution(mesh):
    placed = (
        P("fsdp", "tensor"),
        P("fsdp", "tensor"),
        P("fsdp", "tensor"),
        P("fsdp", "tensor"),
        P("fsdp", "tensor"),
    )
    return jax.shard_map(
        shards,
        mesh=mesh,
        in_specs=placed,
        out_specs=(
            P("fsdp", "tensor"),
            P("fsdp", "tensor"),
            P("fsdp", "tensor"),
            P("fsdp", "tensor"),
        ),
        check_vma=False,
    )
```

profile of v0, /device:TPU:1, one launch (start us, length us, event | category | flops | bytes accessed | tf_op | source)
XLA Modules:
  0.0 300.2 jit_solution(10579336134550925286)
XLA Ops:
  7.2 0.0 all-gather.3.cloned.1.call-start
  7.2 0.7 all-gather.3.cloned.1.call-update
  7.9 0.0 all-gather.5.cloned.1.call-start
  7.9 0.7 all-gather.5.cloned.1.call-update
  8.6 0.0 reduce-scatter.2.cloned.1.call-start
  8.7 1.2 copy.24
  9.9 0.0 copy-start
  9.9 1.3 copy.25
  11.2 0.0 copy-start.2
  11.2 1.3 copy.28
  12.5 2.9 fusion.32
  15.4 2.3 convolution_convert_fusion
  17.7 0.0 copy-done
  17.7 0.0 copy-done.2
  17.7 119.5 %all-gather.3.cloned.1.call-done = bf16[512,6144]{1,0:T(8,128)(2,1)} async-done(((bf16[512,384]{1,0:T(8,128)(2,1)}), bf16[512,6144]{1,0:T(8,128)(2,1)}) %all-gather.3.cloned.1.call-update) | async-done | bytes 6291472 | tf_op jit(solution)/shard_map/all_gather | solution.py:61
  137.2 7.8 %convolution_bitcast_fusion = f32[6144,384]{0,1:T(8,128)} fusion(bf16[512,384]{0,1:T(8,128)(2,1)S(1)} %bitcast.43, bf16[512,6144]{1,0:T(8,128)(2,1)} %all-gather.3.cloned.1.call-done), kind=kOutput, calls=%fused_computation.2 | convolution fusion | flops 2415919104 | bytes 16121856 | tf_op jit(solution)/shard_map/dot_general | solution.py:70
  145.0 0.0 reduce-scatter.2.cloned.1.call-update
  145.1 34.9 %all-gather.5.cloned.1.call-done = bf16[6144,384]{1,0:T(8,128)(2,1)} async-done(((bf16[384,384]{1,0:T(8,128)(2,1)}), bf16[6144,384]{1,0:T(8,128)(2,1)}) %all-gather.5.cloned.1.call-update) | async-done | bytes 4718608 | tf_op jit(solution)/shard_map/all_gather | solution.py:62
  179.9 0.0 copy-start.4
  180.0 6.9 %convolution_convert_fusion.2 = bf16[512,384]{0,1:T(8,128)(2,1)S(1)} fusion(bf16[512,6144]{1,0:T(8,128)(2,1)} %all-gather.3.cloned.1.call-done, bf16[6144,384]{1,0:T(8,128)(2,1)} %all-gather.5.cloned.1.call-done), kind=kOutput, calls=%fused_computation.19 | convolution fusion | flops 2416115712 | bytes 11403264 | tf_op jit(solution)/shard_map/dot_general | solution.py:63
  186.9 0.0 copy-start.3
  186.9 0.0 copy-done.4
  186.9 0.7 convolution_convert_fusion.1
  187.6 0.1 copy-done.3
  187.6 0.9 copy.37
  188.6 1.6 fusion.33
  190.2 0.0 copy-start.1
  190.2 5.2 %fusion.17 = bf16[3,512,128]{1,2,0:T(8,128)(2,1)} fusion(bf16[512,3,128]{0,2,1:T(8,128)(2,1)} %bitcast.37, f32[3,512,512]{1,2,0:T(8,128)S(1)} %fusion.33, f32[3,512,512]{1,2,0:T(8,128)} %get-tuple-element.13, f32[3,512]{1,0:T(4,128)S(1)} %get-tuple-element.12), kind=kOutput, calls=%fused_computation.15 | convolution fusion | flops 207030272 | bytes 7084032 | tf_op jit(solution)/shard_map/hqk,khe->qhe/dot_general | solution.py:37
  195.4 1.9 copy.35
  197.3 0.0 copy-done.1
  197.3 4.9 %fusion.20 = bf16[3,512,128]{1,2,0:T(8,128)(2,1)} fusion(bf16[512,3,128]{0,2,1:T(8,128)(2,1)S(1)} %bitcast.35, f32[3,512,512]{1,2,0:T(8,128)S(1)} %fusion.33, f32[3,512,512]{1,2,0:T(8,128)} %get-tuple-element.13, f32[3,512]{1,0:T(4,128)S(1)} %get-tuple-element.12), kind=kOutput, calls=%fused_computation.16 | convolution fusion | flops 207030272 | bytes 7084032 | tf_op jit(solution)/shard_map/hqk,qhe->khe/dot_general | solution.py:41
  202.3 1.9 copy.36
  204.2 87.4 %reduce-scatter.2.cloned.1.call-done = f32[384,384]{0,1:T(8,128)} async-done(((f32[6144,384]{0,1:T(8,128)}), f32[384,384]{0,1:T(8,128)}) %reduce-scatter.2.cloned.1.call-update) | async-done | bytes 589840 | tf_op jit(solution)/shard_map/reduce_scatter | solution.py:69
  291.5 2.1 copy.38
Async XLA Ops:
  7.2 130.1 %all-gather.3.cloned.1.call-start = ((), (), s32[]{:S(2)}) async-start(), calls=%async_computation.1 | async-start | bytes 6684672 | tf_op jit(solution)/shard_map/all_gather | solution.py:61
  7.9 172.1 %all-gather.5.cloned.1.call-start = ((), (), s32[]{:S(2)}) async-start(), calls=%async_computation.2 | async-start | bytes 5013504 | tf_op jit(solution)/shard_map/all_gather | solution.py:62
  8.6 282.9 %reduce-scatter.2.cloned.1.call-start = ((), (), s32[]{:S(2)}) async-start(), calls=%async_computation.3 | async-start | bytes 10027008 | tf_op jit(solution)/shard_map/reduce_scatter | solution.py:69
  9.9 7.8 %copy-start = (bf16[512,384]{0,1:T(8,128)(2,1)}, bf16[512,384]{0,1:T(8,128)(2,1)S(1)}, u32[]{:S(2)}) copy-start(bf16[512,384]{0,1:T(8,128)(2,1)S(1)} %copy.24) | copy-start | bytes 1179652
  11.2 6.5 %copy-start.2 = (bf16[512,384]{0,1:T(8,128)(2,1)}, bf16[512,384]{0,1:T(8,128)(2,1)S(1)}, u32[]{:S(2)}) copy-start(bf16[512,384]{0,1:T(8,128)(2,1)S(1)} %copy.25) | copy-start | bytes 1179652
  179.9 7.0 %copy-start.4 = (f32[3,512,512]{1,2,0:T(8,128)S(1)}, f32[3,512,512]{1,2,0:T(8,128)}, u32[]{:S(2)}) copy-start(f32[3,512,512]{1,2,0:T(8,128)} %get-tuple-element.13) | copy-start | bytes 9437188
  186.9 0.7 copy-start.3
  190.2 7.1 %copy-start.1 = (bf16[512,384]{0,1:T(8,128)(2,1)S(1)}, bf16[512,384]{0,1:T(8,128)(2,1)}, u32[]{:S(2)}) copy-start(bf16[512,384]{0,1:T(8,128)(2,1)} %copy-done) | copy-start | bytes 1179652
Sparse Core Ops, SparseCore 0:
  10.5 126.6 all-gather.2
  139.1 40.8 all-gather.4
  182.5 108.9 reduce-scatter.1
where the time goes:
time: 301 us; the launch traced here: 300 us
  waiting for transfers between devices  243 us (81%)
  matrix products  32.3 us (11%)
  between operations  13.9 us (5%)
  local copies, waits for them, and re-layouts  10.7 us (4%)
    all_gather x1, waiting for transfers between devices, shards(): full_grad = lax.all_gather(grad_out, 'tensor', axis=1, tiled=True)  120 us
    reduce_scatter x1, waiting for transfers between devices, shards(): lax.psum_scatter(lax.dot_general(full_grad, attended, (((0,), (0,)), ((),...  87.4 us
    all_gather x1, waiting for transfers between devices, shards(): whole_weight = lax.all_gather(out_weight, 'fsdp', axis=0, tiled=True)  34.9 us
    unnamed x17, local copies, waits for them, and re-layouts  10.7 us
    dot_general x1, matrix products, shards(): lax.dot_general(full_grad, attended, (((0,), (0,)), ((), ())), preferred_...  7.81 us
    dot_general x1, matrix products, shards(): jnp.dot(full_grad, whole_weight, preferred_element_type=jnp.float32)  6.94 us
  transfers between devices with their start and end apart: 3, of which 3 were waited for; matrix products, arithmetic and copies ran while one was open for 14% of the time, Pallas kernels for 0%

commit v1 on v0

v1 whole, which is shorter than its diff:
```python
import functools

import jax
import jax.numpy as jnp
from jax import lax
from jax.experimental import pallas as pl
from jax.experimental.pallas import tpu as pltpu
from jax.sharding import PartitionSpec as P

HEAD_DIM = 128
SCALE = HEAD_DIM ** (-0.5)
MESH = pl.DeviceIdType.MESH
BF = jnp.bfloat16
F32 = jnp.float32
TN = (((0,), (0,)), ((), ()))
NT = (((1,), (1,)), ((), ()))

SEQ = 512
WIDTH = 384
HALF = 192
HEADS = 3
QCHUNK = 256


def dot(a, b):
    return jnp.dot(a, b, preferred_element_type=F32)


def dotg(a, b, dims):
    return lax.dot_general(a, b, dims, preferred_element_type=F32)


def kernel(
    q_ref, k_ref, v_ref, g_ref, w_ref,
    dq_ref, dk_ref, dv_ref, dw_ref,
    at, ag, wg, t2, probs, cacc, csend, crecv, gbuf, dall, dr, xr, fs, yr, fkeep,
    z_s, z_r, a_s, a_r, wp_s, wp_r, wy_s, wy_r, wx_s, wx_r, wc_s, wc_r,
    t_s, t_r, c_s, c_r, dc_s, dc_r, dx_s, dx_r, dy_s, dy_r,
):
    f = lax.axis_index("fsdp")
    t = lax.axis_index("tensor")
    x = lax.div(f, 4)
    yl = lax.rem(lax.div(f, 2), 2)
    c = lax.rem(f, 2)
    h = lax.div(t, 8)
    z = lax.rem(t, 8)
    oh = 1 - h
    oyl = 1 - yl
    oc = 1 - c

    def dev(x_=None, yl_=None, c_=None, h_=None, z_=None):
        x_ = x if x_ is None else x_
        yl_ = yl if yl_ is None else yl_
        c_ = c if c_ is None else c_
        h_ = h if h_ is None else h_
        z_ = z if z_ is None else z_
        return (x_ * 4 + yl_ * 2 + c_, h_ * 8 + z_)

    def zoff(d):
        return lax.rem(z + 8 + d, 8)

    def xoff(d):
        return lax.rem(x + 4 + d, 4)

    def rcopy(src, dst, ssem, rsem, device):
        return pltpu.make_async_remote_copy(
            src_ref=src, dst_ref=dst, send_sem=ssem, recv_sem=rsem,
            device_id=device, device_id_type=MESH,
        )

    peers = [
        dev(z_=zoff(1)), dev(z_=zoff(-1)),
        dev(h_=oh), dev(yl_=oyl), dev(yl_=oyl, h_=oh),
        dev(x_=xoff(1)), dev(x_=xoff(-1)), dev(x_=xoff(2)),
        dev(c_=oc),
    ]
    barrier = pltpu.get_barrier_semaphore()
    for peer in peers:
        pl.semaphore_signal(barrier, inc=1, device_id=peer, device_id_type=MESH)
    pl.semaphore_wait(barrier, len(peers))

    sent = []

    def zcopy(way, k, own):
        src = zoff(-k) if way == 0 else zoff(k)
        piece = h if own else oh
        to = dev(z_=zoff(1)) if way == 0 else dev(z_=zoff(-1))
        i = 2 * k + (0 if own else 1)
        ref = ag.at[src, piece]
        return rcopy(ref, ref, z_s.at[way, i], z_r.at[way, i], to)

    def wblock(x_, yl_, c_=None):
        c_ = c if c_ is None else c_
        return wg.at[lax.rem(x_, 2) * 4 + yl_ * 2 + c_, lax.div(x_, 2)]

    def wycopy():
        ref = wblock(x, yl)
        return rcopy(ref, ref, wy_s.at[0], wy_r.at[0], dev(yl_=oyl))

    def wxcopy(way, i):
        to = dev(x_=xoff(1)) if way == 0 else dev(x_=xoff(-1))
        if i == 0:
            ref = wblock(x, yl)
        elif i == 1:
            ref = wblock(x, oyl)
        else:
            ref = wblock(xoff(-1), yl) if way == 0 else wblock(xoff(1), oyl)
        return rcopy(ref, ref, wx_s.at[way, i], wx_r.at[way, i], to)

    def wccopy(d, own_row):
        ref = wblock(xoff(d), yl if own_row else oyl)
        i = 2 * d + (0 if own_row else 1)
        return rcopy(ref, ref, wc_s.at[i], wc_r.at[i], dev(c_=oc))

    def tcopy(n):
        return rcopy(
            t2.at[:, pl.ds(n * HEAD_DIM, HEAD_DIM)],
            t2.at[:, pl.ds(WIDTH + n * HEAD_DIM, HEAD_DIM)],
            t_s.at[n], t_r.at[n], dev(h_=oh),
        )

    def start(cp):
        cp.start()
        sent.append(cp)

    def forward_head(n):
        cols = slice(n * HEAD_DIM, (n + 1) * HEAD_DIM)
        for i in range(SEQ // QCHUNK):
            rows = slice(i * QCHUNK, (i + 1) * QCHUNK)
            st = dotg(k_ref[:, cols], q_ref[rows, cols], NT) * SCALE
            e = jnp.exp(st - jnp.max(st, axis=0, keepdims=True))
            p = e * (1.0 / jnp.sum(e, axis=0, keepdims=True))
            probs[n, :, rows] = p
            t2[rows, cols] = dotg(p.astype(BF), v_ref[:, cols], TN).astype(BF)
        start(tcopy(n))

    def backward_head(n):
        cols = slice(n * HEAD_DIM, (n + 1) * HEAD_DIM)
        dk = jnp.zeros((SEQ, HEAD_DIM), F32)
        dv = jnp.zeros((SEQ, HEAD_DIM), F32)
        for i in range(SEQ // QCHUNK):
            rows = slice(i * QCHUNK, (i + 1) * QCHUNK)
            p = probs[n, :, rows]
            gh = gbuf[rows, cols]
            gp = dotg(v_ref[:, cols], gh, NT)
            rd = jnp.sum(p * gp, axis=0, keepdims=True)
            ds = (p * (gp - rd) * SCALE).astype(BF)
            dq_ref[rows, cols] = dotg(ds, k_ref[:, cols], TN).astype(BF)
            dk = dk + dot(ds, q_ref[rows, cols])
            dv = dv + dot(p.astype(BF), gh)
        dk_ref[:, cols] = dk.astype(BF)
        dv_ref[:, cols] = dv.astype(BF)

    def dcore(zp):
        s = lax.div(zp, 2)
        return rcopy(dall.at[zp], dr.at[s], dc_s.at[s], dc_r.at[s], dev(c_=oc))

    def dxcopy(zp, yh):
        s = lax.div(zp, 2)
        xj = 2 * yh + lax.div(zp, 4)
        row = lax.rem(s, 2)
        dx = lax.rem(x - xj + 4, 4)
        slot = lax.max(dx - 1, 0)
        return xj, rcopy(
            dall.at[zp, yh], xr.at[row, slot], dx_s.at[s, yh], dx_r.at[row, slot], dev(x_=xj)
        )

    def dproduct(d):
        zp = zoff(d)
        a = ag[zp].reshape(WIDTH, SEQ)
        for i in range(3):
            cols = slice(i * 256, (i + 1) * 256)
            dall[zp, :, :, cols] = dot(a, t2[:, cols]).astype(BF).reshape(2, HALF, 256)

        @pl.when(lax.rem(zp, 2) != c)
        def _():
            dcore(zp).start()

    def dpass(d):
        zp = zoff(d)

        @pl.when(lax.rem(zp, 2) == c)
        def _():
            s = lax.div(zp, 2)
            dcore(zp).wait_recv()
            for yh in range(2):
                dall[zp, yh] = (dall[zp, yh].astype(F32) + dr[s, yh].astype(F32)).astype(BF)
                xj, cp = dxcopy(zp, yh)

                @pl.when(xj != x)
                def _():
                    cp.start()

    def cproduct(d):
        zp = zoff(d)
        a = ag[zp].reshape(WIDTH, SEQ).T
        for i in range(3):
            cols = slice(i * 256, (i + 1) * 256)
            cacc[:, cols] += dot(a, wg[zp, :, :, cols].reshape(WIDTH, 256))

    at[...] = g_ref[...].T.reshape(2, HALF, SEQ)
    acopy = rcopy(at.at[oh], ag.at[z, h], a_s.at[0], a_r.at[0], dev(h_=oh))
    start(acopy)
    ag[z, h] = at[h]
    for way in range(2):
        start(zcopy(way, 0, True))
    zj = lax.rem(x, 2) * 4 + yl * 2 + c
    yj = lax.div(x, 2)
    wpcopy = rcopy(
        w_ref.at[oh], wg.at[zj, yj, :, pl.ds(WIDTH, WIDTH)], wp_s.at[0], wp_r.at[0], dev(h_=oh)
    )
    start(wpcopy)
    wg[zj, yj, :, 0:WIDTH] = w_ref[h]

    forward_head(0)

    acopy.wait_recv()
    for way in range(2):
        start(zcopy(way, 0, False))
    wpcopy.wait_recv()
    start(wycopy())
    for way in range(2):
        start(wxcopy(way, 0))
    start(wccopy(0, True))

    forward_head(1)

    def zround(k, own):
        for way in range(2):
            zcopy(way, k, own).wait_recv()
            if k < 2 or (way == 0) == own:
                start(zcopy(way, k + 1, own))

    zround(0, True)
    forward_head(2)
    wycopy().wait_recv()
    for way in range(2):
        start(wxcopy(way, 1))
    start(wccopy(0, False))
    zround(0, False)
    for way, d in ((0, 3), (1, 1)):
        wxcopy(way, 0).wait_recv()
        if way == 0:
            start(wxcopy(way, 2))
        start(wccopy(d, True))
    zround(1, True)
    for n in range(HEADS):
        tcopy(n).wait_recv()
    dproduct(0)
    zround(1, False)
    dproduct(1)
    dproduct(-1)
    for way, d in ((0, 3), (1, 1)):
        wxcopy(way, 1).wait_recv()
        if way == 1:
            start(wxcopy(way, 2))
        start(wccopy(d, False))
    dpass(0)
    zround(2, True)
    dpass(1)
    dpass(-1)
    dproduct(2)
    dproduct(-2)
    zround(2, False)
    dpass(2)
    dpass(-2)
    dproduct(3)
    dproduct(-3)
    wxcopy(0, 2).wait_recv()
    start(wccopy(2, True))
    wxcopy(1, 2).wait_recv()
    start(wccopy(2, False))
    dpass(3)
    dpass(-3)
    for d in range(4):
        for own_row in (True, False):
            wccopy(d, own_row).wait_recv()
    cacc[...] = jnp.zeros_like(cacc)

    @pl.loop(-3, 4)
    def _(d):
        cproduct(d)

    zcopy(0, 3, True).wait_recv()
    zcopy(1, 3, False).wait_recv()
    cproduct(4)
    csend[...] = cacc[:, WIDTH : 2 * WIDTH].astype(BF)
    ccopy = rcopy(csend, crecv, c_s.at[0], c_r.at[0], dev(h_=oh))
    start(ccopy)
    dproduct(4)
    dpass(4)
    ccopy.wait_recv()
    gbuf[...] = (cacc[:, 0:WIDTH] + crecv[...].astype(F32)).astype(BF)
    backward_head(0)

    def total(row):
        zf = lax.rem(x, 2) * 4 + row * 2 + c
        yh = lax.div(x, 2)
        for i in range(3):
            rcopy(xr.at[row, i], xr.at[row, i], dx_s.at[0, 0], dx_r.at[row, i], dev(x_=xoff(1))).wait_recv()
        acc = dall[zf, yh].astype(F32)
        for i in range(3):
            acc = acc + xr[row, i].astype(F32)
        return acc

    def ycopy(i):
        to = (dev(yl_=oyl), dev(yl_=oyl, h_=oh), dev(h_=oh))[i]
        return rcopy(fs.at[i], yr.at[i], dy_s.at[i], dy_r.at[i], to)

    other = total(oyl)
    fs[0] = other[:, 0:WIDTH].astype(BF)
    fs[1] = other[:, WIDTH:].astype(BF)
    start(ycopy(0))
    start(ycopy(1))
    mine = total(yl)
    fs[2] = mine[:, WIDTH:].astype(BF)
    start(ycopy(2))
    fkeep[...] = mine[:, 0:WIDTH]
    backward_head(1)
    backward_head(2)
    for i in range(3):
        ycopy(i).wait_recv()
    dw_ref[h] = fkeep[...] + yr[0].astype(F32)
    dw_ref[oh] = yr[1].astype(F32) + yr[2].astype(F32)

    for cp in sent:
        cp.wait_send()
    for s in range(4):
        dcore(2 * s + oc).wait_send()
        for yh in range(2):
            xj, cp = dxcopy(2 * s + c, yh)

            @pl.when(xj != x)
            def _():
                cp.wait_send()


def shards(queries, keys, values, grad_out, out_weight):
    vmem = pl.BlockSpec(memory_space=pltpu.VMEM)
    dma = pltpu.SemaphoreType.DMA
    pairs = [
        (2, 8), (1,), (1,), (1,), (2, 3), (8,),
        (3,), (1,),
    ]
    sems = []
    for shape in pairs:
        sems += [dma(shape), dma(shape)]
    sems += [dma((4,)), dma((4,)), dma((4, 2)), dma((2, 3)), dma((3,)), dma((3,))]
    d_queries, d_keys, d_values, d_weight = pl.pallas_call(
        kernel,
        out_shape=(
            jax.ShapeDtypeStruct((SEQ, WIDTH), BF),
            jax.ShapeDtypeStruct((SEQ, WIDTH), BF),
            jax.ShapeDtypeStruct((SEQ, WIDTH), BF),
            jax.ShapeDtypeStruct((2, HALF, WIDTH), F32),
        ),
        in_specs=[vmem] * 5,
        out_specs=(vmem,) * 4,
        scratch_shapes=[
            pltpu.VMEM((2, HALF, SEQ), BF),
            pltpu.VMEM((8, 2, HALF, SEQ), BF),
            pltpu.VMEM((8, 2, HALF, 2 * WIDTH), BF),
            pltpu.VMEM((SEQ, 2 * WIDTH), BF),
            pltpu.VMEM((HEADS, SEQ, SEQ), F32),
            pltpu.VMEM((SEQ, 2 * WIDTH), F32),
            pltpu.VMEM((SEQ, WIDTH), BF),
            pltpu.VMEM((SEQ, WIDTH), BF),
            pltpu.VMEM((SEQ, WIDTH), BF),
            pltpu.VMEM((8, 2, HALF, 2 * WIDTH), BF),
            pltpu.VMEM((4, 2, HALF, 2 * WIDTH), BF),
            pltpu.VMEM((2, 3, HALF, 2 * WIDTH), BF),
            pltpu.VMEM((3, HALF, WIDTH), BF),
            pltpu.VMEM((3, HALF, WIDTH), BF),
            pltpu.VMEM((HALF, WIDTH), F32),
        ]
        + sems,
        compiler_params=pltpu.CompilerParams(
            collective_id=1, has_side_effects=True, vmem_limit_bytes=48 << 20
        ),
        cost_estimate=pl.CostEstimate(
            flops=6_000_000_000, bytes_accessed=4_000_000, transcendentals=800_000
        ),
    )(queries, keys, values, grad_out, out_weight.reshape(2, HALF, WIDTH))
    return d_queries, d_keys, d_values, d_weight.reshape(WIDTH, WIDTH)


def solution(mesh):
    placed = P("fsdp", "tensor")
    return jax.shard_map(
        shards,
        mesh=mesh,
        in_specs=(placed,) * 5,
        out_specs=(placed,) * 4,
        check_vma=False,
    )
```

time: 301 us -> 91 us (0.30)
  the two profiles are of different devices: /device:TPU:1 before, /device:TPU:166 now
where the time goes in v1:
time: 91 us; the launch traced here: 90.7 us
  Pallas kernels  82.1 us (90%)
  local copies, waits for them, and re-layouts  7.99 us (9%)
    pallas_call x1, Pallas kernels, shards(): pl.pallas_call(kernel, out_shape=(jax.ShapeDtypeStruct((SEQ, WIDTH), BF),...  82.1 us
    unnamed x14, local copies, waits for them, and re-layouts  7.99 us

profile of v1, /device:TPU:166, one launch (start us, length us, event | category | flops | bytes accessed | tf_op | source)
XLA Modules:
  0.0 90.7 jit_solution(17463642279608742174)
XLA Ops:
  0.6 0.0 copy-start
  0.6 1.0 %copy-done = bf16[512,384]{1,0:T(8,128)(2,1)S(1)} copy-done((bf16[512,384]{1,0:T(8,128)(2,1)S(1)}, bf16[512,384]{1,0:T(8,128)(2,1)}, u32[]{:S(2)}) %copy-start) | copy-done | bytes 393240
  1.6 0.0 copy-start.1
  1.6 1.0 %copy-done.1 = bf16[512,384]{1,0:T(8,128)(2,1)S(1)} copy-done((bf16[512,384]{1,0:T(8,128)(2,1)S(1)}, bf16[512,384]{1,0:T(8,128)(2,1)}, u32[]{:S(2)}) %copy-start.1) | copy-done | bytes 393240
  2.6 0.0 copy-start.2
  2.6 1.0 %copy-done.2 = bf16[512,384]{1,0:T(8,128)(2,1)S(1)} copy-done((bf16[512,384]{1,0:T(8,128)(2,1)S(1)}, bf16[512,384]{1,0:T(8,128)(2,1)}, u32[]{:S(2)}) %copy-start.2) | copy-done | bytes 393240
  3.6 0.0 copy-start.3
  3.6 1.0 %copy-done.3 = bf16[512,384]{1,0:T(8,128)(2,1)S(1)} copy-done((bf16[512,384]{1,0:T(8,128)(2,1)S(1)}, bf16[512,384]{1,0:T(8,128)(2,1)}, u32[]{:S(2)}) %copy-start.3) | copy-done | bytes 393240
  4.6 0.0 copy-start.4
  4.6 1.0 %copy-done.4 = bf16[384,384]{1,0:T(8,128)(2,1)S(1)} copy-done((bf16[384,384]{1,0:T(8,128)(2,1)S(1)}, bf16[384,384]{1,0:T(8,128)(2,1)}, u32[]{:S(2)}) %copy-start.4) | copy-done | bytes 294936
  5.6 82.1 %shard_map.84 = (bf16[512,384]{1,0:T(8,128)(2,1)S(1)}, bf16[512,384]{1,0:T(8,128)(2,1)S(1)}, bf16[512,384]{1,0:T(8,128)(2,1)S(1)}, f32[2,192,384]{2,1,0:T(8,128)S(1)}) custom-call(bf16[512,384]{1,0:T(8,128)(2,1)S(1)} %copy-done, bf16[512,384]{1,0:T(8,128)(2,1)S(1)} %copy-done.1, bf16[512,384]{1,0:T(8,128)(2,1)S(1)} %copy-done.2, ...), custom_call_target="tpu_custom_call" | custom-call | flops 6000000000 | bytes 4000000 | tf_op jit(solution)/shard_map/pallas_call | solution.py:349
  87.7 0.7 copy.13
  88.4 0.7 copy.14
  89.2 0.7 copy.15
  89.9 0.8 copy.16
Async XLA Ops:
  0.6 1.0 %copy-start = (bf16[512,384]{1,0:T(8,128)(2,1)S(1)}, bf16[512,384]{1,0:T(8,128)(2,1)}, u32[]{:S(2)}) copy-start(bf16[512,384]{1,0:T(8,128)(2,1)} %q_ref.1) | copy-start | bytes 1179652
  1.6 1.0 %copy-start.1 = (bf16[512,384]{1,0:T(8,128)(2,1)S(1)}, bf16[512,384]{1,0:T(8,128)(2,1)}, u32[]{:S(2)}) copy-start(bf16[512,384]{1,0:T(8,128)(2,1)} %k_ref.1) | copy-start | bytes 1179652
  2.6 1.0 %copy-start.2 = (bf16[512,384]{1,0:T(8,128)(2,1)S(1)}, bf16[512,384]{1,0:T(8,128)(2,1)}, u32[]{:S(2)}) copy-start(bf16[512,384]{1,0:T(8,128)(2,1)} %v_ref.1) | copy-start | bytes 1179652
  3.6 1.0 %copy-start.3 = (bf16[512,384]{1,0:T(8,128)(2,1)S(1)}, bf16[512,384]{1,0:T(8,128)(2,1)}, u32[]{:S(2)}) copy-start(bf16[512,384]{1,0:T(8,128)(2,1)} %g_ref.1) | copy-start | bytes 1179652
  4.6 1.0 %copy-start.4 = (bf16[384,384]{1,0:T(8,128)(2,1)S(1)}, bf16[384,384]{1,0:T(8,128)(2,1)}, u32[]{:S(2)}) copy-start(bf16[384,384]{1,0:T(8,128)(2,1)} %param.9) | copy-start | bytes 884740

commit v2 on v1

v2 whole, which is shorter than its diff:
```python
import functools

import jax
import jax.numpy as jnp
from jax import lax
from jax.experimental import pallas as pl
from jax.experimental.pallas import tpu as pltpu
from jax.sharding import PartitionSpec as P

HEAD_DIM = 128
SCALE = HEAD_DIM ** (-0.5)
MESH = pl.DeviceIdType.MESH
BF = jnp.bfloat16
F32 = jnp.float32
TN = (((0,), (0,)), ((), ()))
NT = (((1,), (1,)), ((), ()))

SEQ = 512
WIDTH = 384
HALF = 192
HEADS = 3
QCHUNK = 256


def dot(a, b):
    return jnp.dot(a, b, preferred_element_type=F32)


def dotg(a, b, dims):
    return lax.dot_general(a, b, dims, preferred_element_type=F32)


def kernel(
    q_hbm, k_hbm, v_hbm, g_hbm, w_hbm,
    dq_ref, dk_ref, dv_ref, dw_ref,
    q_ref, k_ref, v_ref, g_ref, w_ref,
    at, ag, an, wg, t2, probs, cacc, csend, crecv, gbuf, dall, dr, xr, fs, yr, fkeep,
    in_s,
    z_s, z_r, a_s, a_r, wp_s, wp_r, wy_s, wy_r, wx_s, wx_r, wc_s, wc_r,
    t_s, t_r, c_s, c_r, dc_s, dc_r, dx_s, dx_r, dy_s, dy_r,
):
    f = lax.axis_index("fsdp")
    t = lax.axis_index("tensor")
    x = lax.div(f, 4)
    yl = lax.rem(lax.div(f, 2), 2)
    c = lax.rem(f, 2)
    h = lax.div(t, 8)
    z = lax.rem(t, 8)
    oh = 1 - h
    oyl = 1 - yl
    oc = 1 - c

    def dev(x_=None, yl_=None, c_=None, h_=None, z_=None):
        x_ = x if x_ is None else x_
        yl_ = yl if yl_ is None else yl_
        c_ = c if c_ is None else c_
        h_ = h if h_ is None else h_
        z_ = z if z_ is None else z_
        return (x_ * 4 + yl_ * 2 + c_, h_ * 8 + z_)

    def zoff(d):
        return lax.rem(z + 8 + d, 8)

    def xoff(d):
        return lax.rem(x + 4 + d, 4)

    def rcopy(src, dst, ssem, rsem, device):
        return pltpu.make_async_remote_copy(
            src_ref=src, dst_ref=dst, send_sem=ssem, recv_sem=rsem,
            device_id=device, device_id_type=MESH,
        )

    loads = {}
    for i, (name, src, dst) in enumerate((
        ("g", g_hbm, g_ref), ("w", w_hbm, w_ref), ("k", k_hbm, k_ref),
        ("q", q_hbm, q_ref), ("v", v_hbm, v_ref),
    )):
        loads[name] = pltpu.make_async_copy(src, dst, in_s.at[i])
        loads[name].start()

    peers = [
        dev(z_=zoff(1)), dev(z_=zoff(-1)),
        dev(h_=oh), dev(yl_=oyl), dev(yl_=oyl, h_=oh),
        dev(x_=xoff(1)), dev(x_=xoff(-1)), dev(x_=xoff(2)),
        dev(c_=oc),
    ]
    barrier = pltpu.get_barrier_semaphore()
    for peer in peers:
        pl.semaphore_signal(barrier, inc=1, device_id=peer, device_id_type=MESH)

    sent = []

    def start(cp):
        cp.start()
        sent.append(cp)

    def zcopy(way, k, own):
        src = zoff(-k) if way == 0 else zoff(k)
        piece = h if own else oh
        to = dev(z_=zoff(1)) if way == 0 else dev(z_=zoff(-1))
        i = 2 * k + (0 if own else 1)
        ref = ag.at[src, piece]
        return rcopy(ref, ref, z_s.at[way, i], z_r.at[way, i], to)

    def wblock(x_, yl_, part):
        return wg.at[lax.rem(x_, 2) * 4 + yl_ * 2 + c, part, lax.div(x_, 2)]

    def wycopy(d, part):
        ref = wblock(xoff(d), yl, part)
        return rcopy(ref, ref, wy_s.at[d, part], wy_r.at[d, part], dev(yl_=oyl))

    def wxcopy(way, i, part):
        to = dev(x_=xoff(1)) if way == 0 else dev(x_=xoff(-1))
        if i == 0:
            ref = wblock(x, yl, part)
        elif i == 1:
            ref = wblock(x, oyl, part)
        elif part == 0:
            ref = wblock(xoff(-1), yl, part) if way == 0 else wblock(xoff(1), oyl, part)
        else:
            ref = wblock(xoff(-1 if way == 0 else 1), yl, part)
            ref = ref.at[pl.ds(way * (HALF // 2), HALF // 2)]
        return rcopy(ref, ref, wx_s.at[way, i, part], wx_r.at[way, i, part], to)

    def wccopy(d, own_row, part):
        ref = wblock(xoff(d), yl if own_row else oyl, part)
        i = 2 * d + (0 if own_row else 1)
        return rcopy(ref, ref, wc_s.at[i, part], wc_r.at[i, part], dev(c_=oc))

    def tcopy(n):
        return rcopy(t2.at[n], t2.at[HEADS + n], t_s.at[n], t_r.at[n], dev(h_=oh))

    def ccopy(n):
        return rcopy(csend.at[n], crecv.at[n], c_s.at[n], c_r.at[n], dev(h_=oh))

    def forward_head(n):
        cols = slice(n * HEAD_DIM, (n + 1) * HEAD_DIM)
        for i in range(SEQ // QCHUNK):
            rows = slice(i * QCHUNK, (i + 1) * QCHUNK)
            st = dotg(k_ref[:, cols], q_ref[rows, cols], NT) * SCALE
            e = jnp.exp(st - jnp.max(st, axis=0, keepdims=True))
            p = e * (1.0 / jnp.sum(e, axis=0, keepdims=True))
            probs[n, :, rows] = p
            t2[n, rows] = dotg(p.astype(BF), v_ref[:, cols], TN).astype(BF)
        start(tcopy(n))

    def backward_head(n):
        cols = slice(n * HEAD_DIM, (n + 1) * HEAD_DIM)
        ccopy(n).wait_recv()
        gbuf[:, cols] = (cacc[0, :, cols] + crecv[n].astype(F32)).astype(BF)
        dk = jnp.zeros((SEQ, HEAD_DIM), F32)
        dv = jnp.zeros((SEQ, HEAD_DIM), F32)
        for i in range(SEQ // QCHUNK):
            rows = slice(i * QCHUNK, (i + 1) * QCHUNK)
            p = probs[n, :, rows]
            gh = gbuf[rows, cols]
            gp = dotg(v_ref[:, cols], gh, NT)
            rd = jnp.sum(p * gp, axis=0, keepdims=True)
            ds = (p * (gp - rd) * SCALE).astype(BF)
            dq_ref[rows, cols] = dotg(ds, k_ref[:, cols], TN).astype(BF)
            dk = dk + dot(ds, q_ref[rows, cols])
            dv = dv + dot(p.astype(BF), gh)
        dk_ref[:, cols] = dk.astype(BF)
        dv_ref[:, cols] = dv.astype(BF)

    def dcore(zp, part):
        s = lax.div(zp, 2)
        return rcopy(
            dall.at[zp, part], dr.at[s, part], dc_s.at[s, part], dc_r.at[s, part], dev(c_=oc)
        )

    def dxcopy(zp, part, yh):
        s = lax.div(zp, 2)
        xj = 2 * yh + lax.div(zp, 4)
        row = lax.rem(s, 2)
        slot = lax.max(lax.rem(x - xj + 4, 4) - 1, 0)
        return xj, rcopy(
            dall.at[zp, part, yh], xr.at[row, slot, part],
            dx_s.at[s, part, yh], dx_r.at[row, slot, part], dev(x_=xj),
        )

    def dproduct(part, *ds):
        b = jnp.concatenate([t2[part * HEADS + n] for n in range(HEADS)], axis=1)
        for d in ds:
            zp = zoff(d)
            for yh in range(2):
                dall[zp, part, yh] = dot(ag[zp, yh], b).astype(BF)

            @pl.when(lax.rem(zp, 2) != c)
            def _():
                dcore(zp, part).start()

    def dpass(part, *ds):
        for d in ds:
            zp = zoff(d)

            @pl.when(lax.rem(zp, 2) == c)
            def _():
                s = lax.div(zp, 2)
                dcore(zp, part).wait_recv()
                for yh in range(2):
                    dall[zp, part, yh] = (
                        dall[zp, part, yh].astype(F32) + dr[s, part, yh].astype(F32)
                    ).astype(BF)
                    xj, cp = dxcopy(zp, part, yh)

                    @pl.when(xj != x)
                    def _():
                        cp.start()

    def total(row, part):
        zf = lax.rem(x, 2) * 4 + row * 2 + c
        yh = lax.div(x, 2)
        acc = dall[zf, part, yh].astype(F32)
        for i in range(3):
            rcopy(
                xr.at[row, i, part], xr.at[row, i, part], dx_s.at[0, 0, 0],
                dx_r.at[row, i, part], dev(x_=xoff(1)),
            ).wait_recv()
            acc = acc + xr[row, i, part].astype(F32)
        return acc

    def ycopy(i):
        to = (dev(yl_=oyl), dev(yl_=oyl, h_=oh), dev(h_=oh))[i]
        return rcopy(fs.at[i], yr.at[i], dy_s.at[i], dy_r.at[i], to)

    def transposed(d):
        zp = zoff(d)
        an[zp] = ag[zp].reshape(WIDTH, SEQ).T

    def cproduct(part, ds):
        for i in range(2):
            rows = slice(i * 256, (i + 1) * 256)
            acc = cacc[part, rows]
            for d in ds:
                zp = zoff(d)
                acc = acc + dot(an[zp, rows], wg[zp, part].reshape(WIDTH, WIDTH))
            cacc[part, rows] = acc

    def zround(k, own):
        for way in range(2):
            zcopy(way, k, own).wait_recv()
            if k < 2 or (way == 0) == own:
                start(zcopy(way, k + 1, own))

    def wrow():
        wycopy(0, 0).wait_recv()
        for way in range(2):
            start(wxcopy(way, 1, 0))
        start(wccopy(0, False, 0))

    def wnear(i):
        for way, d in ((0, 3), (1, 1)):
            wxcopy(way, i, 0).wait_recv()
            if way == i:
                start(wxcopy(way, 2, 0))
            start(wccopy(d, i == 0, 0))

    def wfar():
        for way in range(2):
            wxcopy(way, 2, 0).wait_recv()
            start(wccopy(2, way == 0, 0))

    def wpartner():
        wpcopy.wait_recv()
        for way in range(2):
            start(wxcopy(way, 0, 1))
        start(wycopy(0, 1))
        start(wccopy(0, True, 1))

    def pnear():
        for way, d in ((0, 3), (1, 1)):
            wxcopy(way, 0, 1).wait_recv()
            start(wxcopy(way, 2, 1))
            start(wycopy(d, 1))
            start(wccopy(d, True, 1))

    def pfar():
        for way in range(2):
            wxcopy(way, 2, 1).wait_recv()
        start(wycopy(2, 1))
        start(wccopy(2, True, 1))

    def prow():
        for d in (0, 3, 1, 2):
            wycopy(d, 1).wait_recv()
            start(wccopy(d, False, 1))

    def tready():
        for n in range(HEADS):
            tcopy(n).wait_recv()

    def wdone(part):
        for d in range(4):
            for own_row in (True, False):
                wccopy(d, own_row, part).wait_recv()

    def zlast():
        zcopy(0, 3, True).wait_recv()
        zcopy(1, 3, False).wait_recv()

    zj = lax.rem(x, 2) * 4 + yl * 2 + c
    yj = lax.div(x, 2)
    loads["g"].wait()
    at[...] = g_ref[...].T.reshape(2, HALF, SEQ)
    ag[z, h] = at[h]
    loads["w"].wait()
    wg[zj, 0, yj] = w_ref[h]
    pl.semaphore_wait(barrier, len(peers))

    acopy = rcopy(at.at[oh], ag.at[z, h], a_s.at[0], a_r.at[0], dev(h_=oh))
    start(acopy)
    start(wycopy(0, 0))
    for way in range(2):
        start(zcopy(way, 0, True))
        start(wxcopy(way, 0, 0))
    wpcopy = rcopy(w_ref.at[oh], wg.at[zj, 1, yj], wp_s.at[0], wp_r.at[0], dev(h_=oh))
    start(wpcopy)
    start(wccopy(0, True, 0))

    for name in ("k", "q", "v"):
        loads[name].wait()
    forward_head(0)
    forward_head(1)
    forward_head(2)
    cacc[...] = jnp.zeros_like(cacc)
    zround(0, True)
    wrow()
    wnear(0)
    acopy.wait_recv()
    for way in range(2):
        start(zcopy(way, 0, False))
    dproduct(0, 0)
    wnear(1)
    zround(1, True)
    wpartner()
    dpass(0, 0)
    zround(0, False)
    dproduct(0, 1, -1)
    wfar()
    transposed(0)
    zround(2, True)
    dpass(0, 1, -1)
    pnear()
    zround(1, False)
    dproduct(0, 2, -2)
    transposed(1)
    transposed(-1)
    tready()
    dproduct(1, 0, 1, -1)
    dpass(0, 2, -2)
    pfar()
    dpass(1, 0)
    dproduct(1, 2, -2)
    dpass(1, 1, -1)
    zround(2, False)
    dproduct(0, 3, -3)
    dpass(1, 2, -2)
    dproduct(1, 3, -3)
    transposed(2)
    transposed(-2)
    dpass(0, 3, -3)
    wdone(0)
    cproduct(0, range(-2, 3))
    transposed(3)
    transposed(-3)
    dpass(1, 3, -3)
    prow()
    wdone(1)
    cproduct(1, range(-3, 4))
    zlast()
    transposed(4)
    cproduct(1, [4])
    for n in range(HEADS):
        csend[n] = cacc[1, :, pl.ds(n * HEAD_DIM, HEAD_DIM)].astype(BF)
        start(ccopy(n))
    dproduct(0, 4)
    dproduct(1, 4)
    cproduct(0, [-3, 3, 4])
    dpass(0, 4)
    dpass(1, 4)
    backward_head(0)
    fs[0] = total(oyl, 0).astype(BF)
    start(ycopy(0))
    fs[1] = total(oyl, 1).astype(BF)
    start(ycopy(1))
    fs[2] = total(yl, 1).astype(BF)
    start(ycopy(2))
    backward_head(1)
    fkeep[...] = total(yl, 0)
    backward_head(2)
    for i in range(3):
        ycopy(i).wait_recv()
    dw_ref[h] = fkeep[...] + yr[0].astype(F32)
    dw_ref[oh] = yr[1].astype(F32) + yr[2].astype(F32)

    for cp in sent:
        cp.wait_send()
    for s in range(4):
        for part in range(2):
            dcore(2 * s + oc, part).wait_send()
            for yh in range(2):
                xj, cp = dxcopy(2 * s + c, part, yh)

                @pl.when(xj != x)
                def _():
                    cp.wait_send()


def shards(queries, keys, values, grad_out, out_weight):
    vmem = pl.BlockSpec(memory_space=pltpu.VMEM)
    hbm = pl.BlockSpec(memory_space=pltpu.HBM)
    dma = pltpu.SemaphoreType.DMA
    pairs = [
        (2, 8), (1,), (1,), (4, 2), (2, 3, 2), (8, 2),
        (3,), (3,), (4, 2),
    ]
    sems = [dma((5,))]
    for shape in pairs:
        sems += [dma(shape), dma(shape)]
    sems += [dma((4, 2, 2)), dma((2, 3, 2)), dma((3,)), dma((3,))]
    block = pltpu.VMEM((SEQ, WIDTH), BF)
    operands = (queries, keys, values, grad_out, out_weight.reshape(2, HALF, WIDTH))
    operands = [pltpu.with_memory_space_constraint(a, pltpu.HBM) for a in operands]
    d_queries, d_keys, d_values, d_weight = pl.pallas_call(
        kernel,
        out_shape=(
            jax.ShapeDtypeStruct((SEQ, WIDTH), BF),
            jax.ShapeDtypeStruct((SEQ, WIDTH), BF),
            jax.ShapeDtypeStruct((SEQ, WIDTH), BF),
            jax.ShapeDtypeStruct((2, HALF, WIDTH), F32),
        ),
        in_specs=[hbm] * 5,
        out_specs=(vmem,) * 4,
        scratch_shapes=[
            block,
            block,
            block,
            block,
            pltpu.VMEM((2, HALF, WIDTH), BF),
            pltpu.VMEM((2, HALF, SEQ), BF),
            pltpu.VMEM((8, 2, HALF, SEQ), BF),
            pltpu.VMEM((8, SEQ, WIDTH), BF),
            pltpu.VMEM((8, 2, 2, HALF, WIDTH), BF),
            pltpu.VMEM((2 * HEADS, SEQ, HEAD_DIM), BF),
            pltpu.VMEM((HEADS, SEQ, SEQ), F32),
            pltpu.VMEM((2, SEQ, WIDTH), F32),
            pltpu.VMEM((HEADS, SEQ, HEAD_DIM), BF),
            pltpu.VMEM((HEADS, SEQ, HEAD_DIM), BF),
            block,
            pltpu.VMEM((8, 2, 2, HALF, WIDTH), BF),
            pltpu.VMEM((4, 2, 2, HALF, WIDTH), BF),
            pltpu.VMEM((2, 3, 2, HALF, WIDTH), BF),
            pltpu.VMEM((3, HALF, WIDTH), BF),
            pltpu.VMEM((3, HALF, WIDTH), BF),
            pltpu.VMEM((HALF, WIDTH), F32),
        ]
        + sems,
        compiler_params=pltpu.CompilerParams(
            collective_id=1, has_side_effects=True, vmem_limit_bytes=44 << 20
        ),
        cost_estimate=pl.CostEstimate(
            flops=6_000_000_000, bytes_accessed=4_000_000, transcendentals=800_000
        ),
    )(*operands)
    return d_queries, d_keys, d_values, d_weight.reshape(WIDTH, WIDTH)


def solution(mesh):
    placed = P("fsdp", "tensor")
    return jax.shard_map(
        shards,
        mesh=mesh,
        in_specs=(placed,) * 5,
        out_specs=(placed,) * 4,
        check_vma=False,
    )
```

time: 91 us -> 81.6 us (0.90)
  the two profiles are of different devices: /device:TPU:166 before, /device:TPU:38 now
where the time goes in v2:
time: 81.6 us; the launch traced here: 81.5 us
  Pallas kernels  77.8 us (95%)
  local copies, waits for them, and re-layouts  3.05 us (4%)
    pallas_call x1, Pallas kernels, shards(): pl.pallas_call(kernel, out_shape=(jax.ShapeDtypeStruct((SEQ, WIDTH), BF),...  77.8 us
    unnamed x4, local copies, waits for them, and re-layouts  3.05 us

profile of v2, /device:TPU:38, one launch (start us, length us, event | category | flops | bytes accessed | tf_op | source)
XLA Modules:
  0.0 81.5 jit_solution(13531334856007489907)
XLA Ops:
  0.6 77.8 %shard_map.84 = (bf16[512,384]{1,0:T(8,128)(2,1)S(1)}, bf16[512,384]{1,0:T(8,128)(2,1)S(1)}, bf16[512,384]{1,0:T(8,128)(2,1)S(1)}, f32[2,192,384]{2,1,0:T(8,128)S(1)}) custom-call(bf16[512,384]{1,0:T(8,128)(2,1)} %q_hbm.1, bf16[512,384]{1,0:T(8,128)(2,1)} %k_hbm.1, bf16[512,384]{1,0:T(8,128)(2,1)} %v_hbm.1, bf16[512,384]{1,0:T(8,128)(2,1)} %g_hbm.1, ...), custom_call_target="tpu_custom_call" | custom-call | flops 6000000000 | bytes 4000000 | tf_op jit(solution)/shard_map/pallas_call | solution.py:425
  78.4 0.7 copy.13
  79.1 0.7 copy.14
  79.9 0.7 copy.15
  80.6 0.8 copy.16

commit v3 on v2

--- a/solution.py
+++ b/solution.py
@@ -18,6 +18,7 @@
 SEQ = 512
 WIDTH = 384
 HALF = 192
+RELAYED = (0, 1, -1, 2, -2)
 HEADS = 3
 QCHUNK = 256
 
@@ -34,10 +35,10 @@
     q_hbm, k_hbm, v_hbm, g_hbm, w_hbm,
     dq_ref, dk_ref, dv_ref, dw_ref,
     q_ref, k_ref, v_ref, g_ref, w_ref,
-    at, ag, an, wg, t2, probs, cacc, csend, crecv, gbuf, dall, dr, xr, fs, yr, fkeep,
+    at, ag, an, wg, t2, probs, cacc, csend, crecv, gbuf, dall, dr, xp, xr, fs, yr, fkeep,
     in_s,
     z_s, z_r, a_s, a_r, wp_s, wp_r, wy_s, wy_r, wx_s, wx_r, wc_s, wc_r,
-    t_s, t_r, c_s, c_r, dc_s, dc_r, dx_s, dx_r, dy_s, dy_r,
+    t_s, t_r, c_s, c_r, dc_s, dc_r, dp_s, dp_r, dx_s, dx_r, dy_s, dy_r,
 ):
     f = lax.axis_index("fsdp")
     t = lax.axis_index("tensor")
@@ -94,12 +95,15 @@
         cp.start()
         sent.append(cp)
 
-    def zcopy(way, k, own):
+    def zcopy(way, k, half):
         src = zoff(-k) if way == 0 else zoff(k)
-        piece = h if own else oh
         to = dev(z_=zoff(1)) if way == 0 else dev(z_=zoff(-1))
-        i = 2 * k + (0 if own else 1)
-        ref = ag.at[src, piece]
+        if half is None:
+            i = 8 + k
+            ref = ag.at[src, oh]
+        else:
+            i = 2 * k + half
+            ref = ag.at[src, h, pl.ds(half * (HALF // 2), HALF // 2)]
         return rcopy(ref, ref, z_s.at[way, i], z_r.at[way, i], to)
 
     def wblock(x_, yl_, part):
@@ -108,6 +112,11 @@
     def wycopy(d, part):
         ref = wblock(xoff(d), yl, part)
         return rcopy(ref, ref, wy_s.at[d, part], wy_r.at[d, part], dev(yl_=oyl))
+
+    def wpcopy(same_row):
+        i = 0 if same_row else 1
+        to = dev(h_=oh) if same_row else dev(yl_=oyl, h_=oh)
+        return rcopy(w_ref.at[oh], wblock(x, yl, 1), wp_s.at[i], wp_r.at[i], to)
 
     def wxcopy(way, i, part):
         to = dev(x_=xoff(1)) if way == 0 else dev(x_=xoff(-1))
@@ -190,6 +199,20 @@
             def _():
                 dcore(zp, part).start()
 
+    def even(zp):
+        return lax.rem(x, 2) == lax.div(zp, 4)
+
+    def is_relayed(d):
+        return d in RELAYED
+
+    def dpcopy(zp, d, part, half):
+        i = RELAYED.index(d)
+        src = dall.at[zp, part, 1 - lax.div(x, 2), pl.ds(half * (HALF // 2), HALF // 2)]
+        to = dev(x_=xoff(-1)) if half == 0 else dev(x_=xoff(1))
+        return rcopy(
+            src, xp.at[i, part, half], dp_s.at[i, part, half], dp_r.at[i, part, half], to
+        )
+
     def dpass(part, *ds):
         for d in ds:
             zp = zoff(d)
@@ -202,21 +225,60 @@
                     dall[zp, part, yh] = (
                         dall[zp, part, yh].astype(F32) + dr[s, part, yh].astype(F32)
                     ).astype(BF)
-                    xj, cp = dxcopy(zp, part, yh)
-
-                    @pl.when(xj != x)
+                    if not is_relayed(d):
+                        xj, cp = dxcopy(zp, part, yh)
+
+                        @pl.when(xj != x)
+                        def _():
+                            cp.start()
+
+                if is_relayed(d):
+
+                    @pl.when(even(zp))
                     def _():
-                        cp.start()
+                        for half in range(2):
+                            dpcopy(zp, d, part, half).start()
+
+    def drelay(part, *ds):
+        for d in ds:
+            zp = zoff(d)
+
+            @pl.when((lax.rem(zp, 2) == c) & jnp.logical_not(even(zp)))
+            def _():
+                for half in range(2):
+                    dpcopy(zp, d, part, half).wait_recv()
+                    yh = lax.div(xoff(-1) if half == 0 else xoff(1), 2)
+                    rows = pl.ds(half * (HALF // 2), HALF // 2)
+                    dall[zp, part, yh, rows] = (
+                        dall[zp, part, yh, rows].astype(F32)
+                        + xp[RELAYED.index(d), part, half].astype(F32)
+                    ).astype(BF)
+                    dxcopy(zp, part, yh)[1].start()
 
     def total(row, part):
         zf = lax.rem(x, 2) * 4 + row * 2 + c
         yh = lax.div(x, 2)
+        away = lax.rem(zf - z + 8, 8)
+        relayed = (away <= 2) | (away >= 6)
+        for i in range(3):
+            arrival = rcopy(
+                xr.at[row, i, part], xr.at[row, i, part], dx_s.at[0, 0, 0],
+                dx_r.at[row, i, part], dev(x_=xoff(1)),
+            )
+            if i == 1:
+
+                @pl.when(jnp.logical_not(relayed))
+                def _():
+                    arrival.wait_recv()
+
+                @pl.when(relayed)
+                def _():
+                    xr[row, 1, part] = jnp.zeros((HALF, WIDTH), BF)
+
+            else:
+                arrival.wait_recv()
         acc = dall[zf, part, yh].astype(F32)
         for i in range(3):
-            rcopy(
-                xr.at[row, i, part], xr.at[row, i, part], dx_s.at[0, 0, 0],
-                dx_r.at[row, i, part], dev(x_=xoff(1)),
-            ).wait_recv()
             acc = acc + xr[row, i, part].astype(F32)
         return acc
 
@@ -238,16 +300,27 @@
             cacc[part, rows] = acc
 
     def zround(k, own):
+        for half in (0, 1) if own else (None,):
+            for way in range(2):
+                zcopy(way, k, half).wait_recv()
+                if k < 2 or (way == 0) == own:
+                    start(zcopy(way, k + 1, half))
+
+    def wsend(own_row, part):
         for way in range(2):
-            zcopy(way, k, own).wait_recv()
-            if k < 2 or (way == 0) == own:
-                start(zcopy(way, k + 1, own))
+            start(wxcopy(way, 0 if own_row else 1, part))
+        start(wccopy(0, own_row, part))
 
     def wrow():
         wycopy(0, 0).wait_recv()
-        for way in range(2):
-            start(wxcopy(way, 1, 0))
-        start(wccopy(0, False, 0))
+        wsend(False, 0)
+
+    def wpartner(same_row):
+        wpcopy(same_row).wait_recv()
+        if same_row:
+            wsend(True, 1)
+        else:
+            start(wccopy(0, False, 1))
 
     def wnear(i):
         for way, d in ((0, 3), (1, 1)):
@@ -261,13 +334,6 @@
             wxcopy(way, 2, 0).wait_recv()
             start(wccopy(2, way == 0, 0))
 
-    def wpartner():
-        wpcopy.wait_recv()
-        for way in range(2):
-            start(wxcopy(way, 0, 1))
-        start(wycopy(0, 1))
-        start(wccopy(0, True, 1))
-
     def pnear():
         for way, d in ((0, 3), (1, 1)):
             wxcopy(way, 0, 1).wait_recv()
@@ -282,7 +348,7 @@
         start(wccopy(2, True, 1))
 
     def prow():
-        for d in (0, 3, 1, 2):
+        for d in (3, 1, 2):
             wycopy(d, 1).wait_recv()
             start(wccopy(d, False, 1))
 
@@ -296,8 +362,9 @@
                 wccopy(d, own_row, part).wait_recv()
 
     def zlast():
-        zcopy(0, 3, True).wait_recv()
-        zcopy(1, 3, False).wait_recv()
+        zcopy(0, 3, 0).wait_recv()
+        zcopy(0, 3, 1).wait_recv()
+        zcopy(1, 3, None).wait_recv()
 
     zj = lax.rem(x, 2) * 4 + yl * 2 + c
     yj = lax.div(x, 2)
@@ -310,12 +377,14 @@
 
     acopy = rcopy(at.at[oh], ag.at[z, h], a_s.at[0], a_r.at[0], dev(h_=oh))
     start(acopy)
+    for half in range(2):
+        for way in range(2):
+            start(zcopy(way, 0, half))
+    for way in range(2):
+        start(wxcopy(way, 0, 0))
     start(wycopy(0, 0))
-    for way in range(2):
-        start(zcopy(way, 0, True))
-        start(wxcopy(way, 0, 0))
-    wpcopy = rcopy(w_ref.at[oh], wg.at[zj, 1, yj], wp_s.at[0], wp_r.at[0], dev(h_=oh))
-    start(wpcopy)
+    start(wpcopy(False))
+    start(wpcopy(True))
     start(wccopy(0, True, 0))
 
     for name in ("k", "q", "v"):
@@ -325,70 +394,74 @@
     forward_head(2)
     cacc[...] = jnp.zeros_like(cacc)
     zround(0, True)
-    wrow()
-    wnear(0)
     acopy.wait_recv()
     for way in range(2):
-        start(zcopy(way, 0, False))
+        start(zcopy(way, 0, None))
+    wpartner(False)
+    wnear(0)
     dproduct(0, 0)
-    wnear(1)
+    wrow()
     zround(1, True)
-    wpartner()
-    dpass(0, 0)
+    wpartner(True)
     zround(0, False)
     dproduct(0, 1, -1)
-    wfar()
+    wnear(1)
+    zround(2, True)
+    pnear()
+    dpass(0, 0)
+    dpass(0, 1, -1)
     transposed(0)
-    zround(2, True)
-    dpass(0, 1, -1)
-    pnear()
     zround(1, False)
     dproduct(0, 2, -2)
     transposed(1)
     transposed(-1)
     tready()
     dproduct(1, 0, 1, -1)
+    pfar()
     dpass(0, 2, -2)
-    pfar()
     dpass(1, 0)
     dproduct(1, 2, -2)
+    wfar()
     dpass(1, 1, -1)
+    drelay(0, 0, 1, -1)
+    transposed(2)
+    transposed(-2)
     zround(2, False)
     dproduct(0, 3, -3)
     dpass(1, 2, -2)
+    drelay(0, 2, -2)
     dproduct(1, 3, -3)
-    transposed(2)
-    transposed(-2)
+    drelay(1, 0, 1, -1)
     dpass(0, 3, -3)
-    wdone(0)
-    cproduct(0, range(-2, 3))
+    dpass(1, 3, -3)
+    drelay(1, 2, -2)
     transposed(3)
     transposed(-3)
-    dpass(1, 3, -3)
     prow()
+    wdone(0)
     wdone(1)
     cproduct(1, range(-3, 4))
     zlast()
     transposed(4)
+    dproduct(0, 4)
     cproduct(1, [4])
     for n in range(HEADS):
         csend[n] = cacc[1, :, pl.ds(n * HEAD_DIM, HEAD_DIM)].astype(BF)
         start(ccopy(n))
-    dproduct(0, 4)
     dproduct(1, 4)
-    cproduct(0, [-3, 3, 4])
     dpass(0, 4)
     dpass(1, 4)
+    cproduct(0, range(-3, 5))
     backward_head(0)
+    backward_head(1)
     fs[0] = total(oyl, 0).astype(BF)
     start(ycopy(0))
     fs[1] = total(oyl, 1).astype(BF)
     start(ycopy(1))
     fs[2] = total(yl, 1).astype(BF)
     start(ycopy(2))
-    backward_head(1)
+    backward_head(2)
     fkeep[...] = total(yl, 0)
-    backward_head(2)
     for i in range(3):
         ycopy(i).wait_recv()
     dw_ref[h] = fkeep[...] + yr[0].astype(F32)
@@ -399,12 +472,25 @@
     for s in range(4):
         for part in range(2):
             dcore(2 * s + oc, part).wait_send()
-            for yh in range(2):
-                xj, cp = dxcopy(2 * s + c, part, yh)
-
-                @pl.when(xj != x)
-                def _():
-                    cp.wait_send()
+    for d in (0, 1, -1, 2, -2, 3, -3, 4):
+        zp = zoff(d)
+        for part in range(2):
+
+            @pl.when(lax.rem(zp, 2) == c)
+            def _():
+                for yh in range(2):
+                    xj, cp = dxcopy(zp, part, yh)
+
+                    @pl.when(jnp.logical_not(even(zp)) if is_relayed(d) else xj != x)
+                    def _():
+                        cp.wait_send()
+
+                if is_relayed(d):
+
+                    @pl.when(even(zp))
+                    def _():
+                        for half in range(2):
+                            dpcopy(zp, d, part, half).wait_send()
 
 
 def shards(queries, keys, values, grad_out, out_weight):
@@ -412,8 +498,8 @@
     hbm = pl.BlockSpec(memory_space=pltpu.HBM)
     dma = pltpu.SemaphoreType.DMA
     pairs = [
-        (2, 8), (1,), (1,), (4, 2), (2, 3, 2), (8, 2),
-        (3,), (3,), (4, 2),
+        (2, 12), (1,), (2,), (4, 2), (2, 3, 2), (8, 2),
+        (3,), (3,), (4, 2), (5, 2, 2),
     ]
     sems = [dma((5,))]
     for shape in pairs:
@@ -450,6 +536,7 @@
             block,
             pltpu.VMEM((8, 2, 2, HALF, WIDTH), BF),
             pltpu.VMEM((4, 2, 2, HALF, WIDTH), BF),
+            pltpu.VMEM((5, 2, 2, HALF // 2, WIDTH), BF),
             pltpu.VMEM((2, 3, 2, HALF, WIDTH), BF),
             pltpu.VMEM((3, HALF, WIDTH), BF),
             pltpu.VMEM((3, HALF, WIDTH), BF),

time: 81.6 us -> 75.3 us (0.923)
  the two profiles are of different devices: /device:TPU:38 before, /device:TPU:1 now
where the time goes in v3:
time: 75.3 us; the launch traced here: 75.2 us
  Pallas kernels  71.6 us (95%)
  local copies, waits for them, and re-layouts  3.05 us (4%)
    pallas_call x1, Pallas kernels, shards(): pl.pallas_call(kernel, out_shape=(jax.ShapeDtypeStruct((SEQ, WIDTH), BF),...  71.6 us
    unnamed x4, local copies, waits for them, and re-layouts  3.05 us

profile of v3, /device:TPU:1, one launch (start us, length us, event | category | flops | bytes accessed | tf_op | source)
XLA Modules:
  0.0 75.2 jit_solution(17307164613121502105)
XLA Ops:
  0.6 71.6 %shard_map.84 = (bf16[512,384]{1,0:T(8,128)(2,1)S(1)}, bf16[512,384]{1,0:T(8,128)(2,1)S(1)}, bf16[512,384]{1,0:T(8,128)(2,1)S(1)}, f32[2,192,384]{2,1,0:T(8,128)S(1)}) custom-call(bf16[512,384]{1,0:T(8,128)(2,1)} %q_hbm.1, bf16[512,384]{1,0:T(8,128)(2,1)} %k_hbm.1, bf16[512,384]{1,0:T(8,128)(2,1)} %v_hbm.1, bf16[512,384]{1,0:T(8,128)(2,1)} %g_hbm.1, ...), custom_call_target="tpu_custom_call" | custom-call | flops 6000000000 | bytes 4000000 | tf_op jit(solution)/shard_map/pallas_call | solution.py:511
  72.2 0.7 copy.13
  72.9 0.7 copy.14
  73.7 0.7 copy.15
  74.4 0.8 %copy.16 = f32[384,384]{1,0:T(8,128)} copy(f32[384,384]{1,0:T(8,128)S(1)} %bitcast.2) | data formatting | bytes 1179648

commit v4 on v3

--- a/solution.py
+++ b/solution.py
@@ -33,7 +33,7 @@
 
 def kernel(
     q_hbm, k_hbm, v_hbm, g_hbm, w_hbm,
-    dq_ref, dk_ref, dv_ref, dw_ref,
+    dqkv_ref, dw_ref,
     q_ref, k_ref, v_ref, g_ref, w_ref,
     at, ag, an, wg, t2, probs, cacc, csend, crecv, gbuf, dall, dr, xp, xr, fs, yr, fkeep,
     in_s,
@@ -166,11 +166,11 @@
             gp = dotg(v_ref[:, cols], gh, NT)
             rd = jnp.sum(p * gp, axis=0, keepdims=True)
             ds = (p * (gp - rd) * SCALE).astype(BF)
-            dq_ref[rows, cols] = dotg(ds, k_ref[:, cols], TN).astype(BF)
+            dqkv_ref[0, rows, cols] = dotg(ds, k_ref[:, cols], TN).astype(BF)
             dk = dk + dot(ds, q_ref[rows, cols])
             dv = dv + dot(p.astype(BF), gh)
-        dk_ref[:, cols] = dk.astype(BF)
-        dv_ref[:, cols] = dv.astype(BF)
+        dqkv_ref[1, :, cols] = dk.astype(BF)
+        dqkv_ref[2, :, cols] = dv.astype(BF)
 
     def dcore(zp, part):
         s = lax.div(zp, 2)
@@ -508,16 +508,14 @@
     block = pltpu.VMEM((SEQ, WIDTH), BF)
     operands = (queries, keys, values, grad_out, out_weight.reshape(2, HALF, WIDTH))
     operands = [pltpu.with_memory_space_constraint(a, pltpu.HBM) for a in operands]
-    d_queries, d_keys, d_values, d_weight = pl.pallas_call(
+    d_attention, d_weight = pl.pallas_call(
         kernel,
         out_shape=(
-            jax.ShapeDtypeStruct((SEQ, WIDTH), BF),
-            jax.ShapeDtypeStruct((SEQ, WIDTH), BF),
-            jax.ShapeDtypeStruct((SEQ, WIDTH), BF),
+            jax.ShapeDtypeStruct((3, SEQ, WIDTH), BF),
             jax.ShapeDtypeStruct((2, HALF, WIDTH), F32),
         ),
         in_specs=[hbm] * 5,
-        out_specs=(vmem,) * 4,
+        out_specs=(vmem,) * 2,
         scratch_shapes=[
             block,
             block,
@@ -550,7 +548,7 @@
             flops=6_000_000_000, bytes_accessed=4_000_000, transcendentals=800_000
         ),
     )(*operands)
-    return d_queries, d_keys, d_values, d_weight.reshape(WIDTH, WIDTH)
+    return d_attention[0], d_attention[1], d_attention[2], d_weight.reshape(WIDTH, WIDTH)
 
 
 def solution(mesh):

time: 75.3 us -> 74.2 us (0.985)
  local copies, waits for them, and re-layouts: 3.05 us -> 1.86 us
    unnamed x4 -> x1, local copies, waits for them, and re-layouts: 3.05 us -> 0.81 us
    squeeze x0 -> x1, local copies, waits for them, and re-layouts: none -> 1.05 us  [shards(): d_attention[2]]
where the time goes in v4:
time: 74.2 us; the launch traced here: 74.1 us
  Pallas kernels  71.6 us (96%)
  local copies, waits for them, and re-layouts  1.86 us (3%)
    pallas_call x1, Pallas kernels, shards(): pl.pallas_call(kernel, out_shape=(jax.ShapeDtypeStruct((3, SEQ, WIDTH), B...  71.6 us

profile of v4, /device:TPU:1, one launch (start us, length us, event | category | flops | bytes accessed | tf_op | source)
XLA Modules:
  0.0 74.1 jit_solution(7999640074663644843)
XLA Ops:
  0.6 71.6 %shard_map.84 = (bf16[3,512,384]{2,1,0:T(8,128)(2,1)S(1)}, f32[2,192,384]{2,1,0:T(8,128)S(1)}) custom-call(bf16[512,384]{1,0:T(8,128)(2,1)} %q_hbm.1, bf16[512,384]{1,0:T(8,128)(2,1)} %k_hbm.1, bf16[512,384]{1,0:T(8,128)(2,1)} %v_hbm.1, bf16[512,384]{1,0:T(8,128)(2,1)} %g_hbm.1, bf16[2,192,384]{2,1,0:T(8,128)(2,1)} %bitcast.9), custom_call_target="tpu_custom_call" | custom-call | flops 6000000000 | bytes 4000000 | tf_op jit(solution)/shard_map/pallas_call | solution.py:511
  72.2 1.0 %slice_bitcast_fusion = (bf16[512,384]{1,0:T(8,128)(2,1)}, bf16[512,384]{1,0:T(8,128)(2,1)}, bf16[512,384]{1,0:T(8,128)(2,1)}) fusion(bf16[3,512,384]{2,1,0:T(8,128)(2,1)S(1)} %get-tuple-element.6), kind=kLoop, calls=%fused_computation | loop fusion | bytes 2359296 | tf_op jit(solution)/shard_map/squeeze | solution.py:551
  73.2 0.8 %copy.10 = f32[384,384]{1,0:T(8,128)} copy(f32[384,384]{1,0:T(8,128)S(1)} %bitcast.8) | data formatting | bytes 1179648

commit v5 on v4

--- a/solution.py
+++ b/solution.py
@@ -453,13 +453,13 @@
     dpass(1, 4)
     cproduct(0, range(-3, 5))
     backward_head(0)
-    backward_head(1)
     fs[0] = total(oyl, 0).astype(BF)
     start(ycopy(0))
     fs[1] = total(oyl, 1).astype(BF)
     start(ycopy(1))
     fs[2] = total(yl, 1).astype(BF)
     start(ycopy(2))
+    backward_head(1)
     backward_head(2)
     fkeep[...] = total(yl, 0)
     for i in range(3):

time: 74.2 us -> 74 us (level); the launches traced: 74.1 us -> 72.7 us
  Pallas kernels: 71.6 us -> 70.2 us
    pallas_call x1, Pallas kernels: 71.6 us -> 70.2 us  [shards(): pl.pallas_call(kernel, out_shape=(jax.ShapeDtypeStruct((3, SEQ, WIDTH), B...]
where the time goes in v5:
time: 74 us; the launch traced here: 72.7 us
  Pallas kernels  70.2 us (95%)
  local copies, waits for them, and re-layouts  1.86 us (3%)
    pallas_call x1, Pallas kernels, shards(): pl.pallas_call(kernel, out_shape=(jax.ShapeDtypeStruct((3, SEQ, WIDTH), B...  70.2 us

profile of v5, /device:TPU:1, one launch (start us, length us, event | category | flops | bytes accessed | tf_op | source)
XLA Modules:
  0.0 72.7 jit_solution(8831793858258457425)
XLA Ops:
  0.6 70.2 %shard_map.84 = (bf16[3,512,384]{2,1,0:T(8,128)(2,1)S(1)}, f32[2,192,384]{2,1,0:T(8,128)S(1)}) custom-call(bf16[512,384]{1,0:T(8,128)(2,1)} %q_hbm.1, bf16[512,384]{1,0:T(8,128)(2,1)} %k_hbm.1, bf16[512,384]{1,0:T(8,128)(2,1)} %v_hbm.1, bf16[512,384]{1,0:T(8,128)(2,1)} %g_hbm.1, bf16[2,192,384]{2,1,0:T(8,128)(2,1)} %bitcast.9), custom_call_target="tpu_custom_call" | custom-call | flops 6000000000 | bytes 4000000 | tf_op jit(solution)/shard_map/pallas_call | solution.py:511
  70.8 1.0 %slice_bitcast_fusion = (bf16[512,384]{1,0:T(8,128)(2,1)}, bf16[512,384]{1,0:T(8,128)(2,1)}, bf16[512,384]{1,0:T(8,128)(2,1)}) fusion(bf16[3,512,384]{2,1,0:T(8,128)(2,1)S(1)} %get-tuple-element.6), kind=kLoop, calls=%fused_computation | loop fusion | bytes 2359296 | tf_op jit(solution)/shard_map/squeeze | solution.py:551
  71.9 0.8 %copy.10 = f32[384,384]{1,0:T(8,128)} copy(f32[384,384]{1,0:T(8,128)S(1)} %bitcast.8) | data formatting | bytes 1179648
